TPU v7x, 32 devices: a whole 2x2x4 slice. The times are simulated.
32 devices in a mesh: freq: 16 (over z, y, x), tp: 2 (over core).
Axes of the slice: x: 2, y: 2, z: 4, core: 2. Of those that a mesh axis runs over, the one named last changes fastest.
Arguments:
- tokens: bfloat16 [16384, 768], P('freq'), may hold values from -6 to 6
- lengths: int32 [16], P('freq'), may hold values from 1 to 1024, 8192 in all
- mixgain: float32 [768], replicated, may hold values from 0.5 to 1.5
- mixbias: float32 [768], replicated, may hold values from -1 to 1
- query_weight: bfloat16 [768, 768], P(None, 'tp'), may hold values from -0.21875 to 0.21875
- key_weight: bfloat16 [768, 768], P(None, 'tp'), may hold values from -0.21875 to 0.21875
- value_weight: bfloat16 [768, 768], P(None, 'tp'), may hold values from -0.21875 to 0.21875
- shift_taps: float32 [4, 768], P(None, 'tp'), may hold values from -3 to 3
- state_coef: float32 [768, 64], P('tp'), may hold values from -0.0625 to 0.0625
- state_rate: float32 [768, 64], P('tp'), may hold values from 0.0005 to 0.05
- state_skip: float32 [768], P('tp'), may hold values from -4 to 4
- out_weight: bfloat16 [768, 768], P('tp'), may hold values from -0.21875 to 0.21875
- feedgain: float32 [768], replicated, may hold values from 0.5 to 1.5
- feedbias: float32 [768], replicated, may hold values from -1 to 1
- up_weight: bfloat16 [768, 3072], P(None, 'tp'), may hold values from -0.21875 to 0.21875
- up_bias: float32 [3072], P('tp'), may hold values from -2.5 to 2.5
- down_weight: bfloat16 [3072, 768], P('tp'), may hold values from -0.109375 to 0.109375
- down_bias: float32 [768], replicated, may hold values from -1.5 to 1.5
- cotangent: bfloat16 [16384, 768], P('freq'), may hold values from -6 to 6
Outputs:
- layer_out: bfloat16 [16384, 768], P('freq')
- tokens_grad: float32 [16384, 768], P('freq')
- mixgain_grad: float32 [768], replicated
- mixbias_grad: float32 [768], replicated
- query_grad: float32 [768, 768], P('freq', 'tp')
- key_grad: float32 [768, 768], P('freq', 'tp')
- value_grad: float32 [768, 768], P('freq', 'tp')
- taps_grad: float32 [4, 768], P(None, 'tp')
- coef_grad: float32 [768, 64], P('tp')
- rate_grad: float32 [768, 64], P('tp')
- skip_grad: float32 [768], P('tp')
- outweight_grad: float32 [768, 768], P('tp', 'freq')
- feedgain_grad: float32 [768], replicated
- feedbias_grad: float32 [768], replicated
- upweight_grad: float32 [768, 3072], P('freq', 'tp')
- upbias_grad: float32 [3072], P('tp')
- downweight_grad: float32 [3072, 768], P('tp', 'freq')
- downbias_grad: float32 [768], replicated
Inputs may be any that keep to these rules, and one draw needn't show every extreme that they name: Sequence s fills the first lengths[s] rows of its slot of 1024 rows; the rest of the slot is padding. The lengths sum to 8192, and one of them is 1024.
All inputs are finite; a program needn't handle non-finite values. No bound on the sum of `lengths` on one device may be relied on, other than what follows from the above.
Results may differ from a plain program's by a relative error of at most 0.0075.
Values sent between devices are 32-bit elements; how exact they have to be, the bound alone decides.
No kernel may reach another device: no remote copies, remote signals or barrier semaphores. Data moves between devices by JAX's collectives and lax.ppermute only.
A program may use at most 192 MiB of HBM per device.

v0:
```python
import math

import jax
import jax.numpy as jnp
from jax import lax
from jax.sharding import PartitionSpec as P

exact_mode = lax.Precision.HIGHEST


def layer_norm(value, gain, bias):
    mean = jnp.mean(value, -1, keepdims=True)
    centered = value - mean
    inverse = lax.rsqrt(jnp.mean(centered * centered, -1, keepdims=True) + 1e-05)
    scaled = centered * inverse
    return (scaled * gain + bias, scaled, inverse)


def norm_back(grad_out, scaled, inverse, gain):
    weighted = grad_out * gain
    return inverse * (
        weighted
        - jnp.mean(weighted, -1, keepdims=True)
        - scaled * jnp.mean(weighted * scaled, -1, keepdims=True)
    )


def inner(left, right):
    return lax.dot_general(
        left, right, (((0,), (0,)), ((), ())), preferred_element_type=jnp.float32
    )


def times_transposed(grad, weight):
    return lax.dot_general(
        grad, weight, (((1,), (1,)), ((), ())), preferred_element_type=jnp.float32
    )


def gelu_slope(value):
    return 0.5 * (1.0 + lax.erf(value * (1.0 / math.sqrt(2.0)))) + value * jnp.exp(
        -0.5 * value * value
    ) * (1.0 / math.sqrt(2.0 * math.pi))


def spectrum(coef, rate, bins, span):
    theta = bins.astype(jnp.float32) * (math.pi / span)
    sign = (1 - 2 * (bins % 2)).astype(jnp.float32)[:, None, None]
    half = jnp.sin(0.5 * theta)[:, None, None]
    decay = jnp.exp(-rate)[None]
    tail = jnp.exp(-rate * span)[None]
    real_den = -jnp.expm1(-rate)[None] + decay * 2.0 * half * half
    imag_den = decay * jnp.sin(theta)[:, None, None]
    scale = coef[None] * (1.0 - tail * sign) / (real_den * real_den + imag_den * imag_den)
    return (jnp.sum(scale * real_den, -1), -jnp.sum(scale * imag_den, -1))


def nyquist(coef, rate, span):
    return jnp.sum(coef * (1.0 - jnp.exp(-rate * span)) / (1.0 + jnp.exp(-rate)), -1)


def blocked_spectrum(coef, rate, bins, span):
    width = bins.shape[0]
    block = min(width, 128)
    real, imag = lax.map(
        lambda piece: spectrum(coef, rate, piece, span), bins.reshape(width // block, block)
    )
    return (real.reshape(width, -1), imag.reshape(width, -1))


def spectrum_grads(coef, rate, bins, span, cot_real, cot_imag):
    width = bins.shape[0]
    block = min(width, 128)
    count = width // block

    def step(carry, piece):
        part_bins, part_real, part_imag = piece
        _, pull = jax.vjp(
            lambda part_coef, part_rate: spectrum(part_coef, part_rate, part_bins, span), coef, rate
        )
        coef_part, rate_part = pull((part_real, part_imag))
        return ((carry[0] + coef_part, carry[1] + rate_part), None)

    start = (jnp.zeros_like(coef), jnp.zeros_like(rate))
    totals, _ = lax.scan(
        step,
        start,
        (
            bins.reshape(count, block),
            cot_real.reshape(count, block, -1),
            cot_imag.reshape(count, block, -1),
        ),
    )
    return totals


def body(
    tokens,
    lengths,
    mixgain,
    mixbias,
    query_weight,
    key_weight,
    value_weight,
    shift_taps,
    state_coef,
    state_rate,
    state_skip,
    out_weight,
    feedgain,
    feedbias,
    up_weight,
    up_bias,
    down_weight,
    down_bias,
    cotangent,
):
    seqs = lengths.shape[0]
    rows = tokens.shape[0]
    span = rows // seqs
    chans = query_weight.shape[1]
    lags = shift_taps.shape[0]
    places = lax.axis_size("freq")
    width = span // places
    period = 2 * span
    positions = jnp.arange(span)
    mask = (positions[None, :] < lengths[:, None]).astype(jnp.float32).reshape(rows, 1)
    mask3 = mask.reshape(seqs, span, 1)
    split = 1 << math.isqrt(period).bit_length() - 1
    while split > 2 and (span % split != 0 or split % 2 != 0):
        split = split // 2
    inner_len = span // split
    group_len = period // split
    high = split // 2
    angle_a = (jnp.arange(group_len)[:, None] * jnp.arange(inner_len)[None, :] % group_len).astype(
        jnp.float32
    ) * (2.0 * math.pi / group_len)
    cos_a = jnp.cos(angle_a)
    sin_a = jnp.sin(angle_a)
    whole_bin = jnp.arange(group_len)[:, None, None] + group_len * jnp.arange(high)[None, :, None]
    angle_b = (whole_bin * jnp.arange(split)[None, None, :] % period).astype(jnp.float32) * (
        2.0 * math.pi / period
    )
    cos_b = jnp.cos(angle_b)
    sin_b = jnp.sin(angle_b)
    fold = jnp.where(positions == 0, 1.0, 2.0).astype(jnp.float32) / period
    alter = (1 - 2 * (positions % 2)).astype(jnp.float32)

    def forward_bins(series):
        grid = series.reshape(seqs, inner_len, split, -1)
        part_real = jnp.einsum("gk,skmc->sgmc", cos_a, grid, precision=exact_mode)
        part_imag = -jnp.einsum("gk,skmc->sgmc", sin_a, grid, precision=exact_mode)
        real = jnp.einsum("ghm,sgmc->shgc", cos_b, part_real, precision=exact_mode) + jnp.einsum(
            "ghm,sgmc->shgc", sin_b, part_imag, precision=exact_mode
        )
        imag = jnp.einsum("ghm,sgmc->shgc", cos_b, part_imag, precision=exact_mode) - jnp.einsum(
            "ghm,sgmc->shgc", sin_b, part_real, precision=exact_mode
        )
        top = jnp.einsum("t,stc->sc", alter, series, precision=exact_mode)
        return (real.reshape(seqs, span, -1), imag.reshape(seqs, span, -1), top)

    def inverse_bins(real, imag, top):
        folded_real = (real * fold[None, :, None]).reshape(seqs, high, group_len, -1)
        folded_imag = (imag * fold[None, :, None]).reshape(seqs, high, group_len, -1)
        mid_real = jnp.einsum(
            "ghm,shgc->sgmc", cos_b, folded_real, precision=exact_mode
        ) - jnp.einsum("ghm,shgc->sgmc", sin_b, folded_imag, precision=exact_mode)
        mid_imag = jnp.einsum(
            "ghm,shgc->sgmc", sin_b, folded_real, precision=exact_mode
        ) + jnp.einsum("ghm,shgc->sgmc", cos_b, folded_imag, precision=exact_mode)
        series = jnp.einsum("gk,sgmc->skmc", cos_a, mid_real, precision=exact_mode) - jnp.einsum(
            "gk,sgmc->skmc", sin_a, mid_imag, precision=exact_mode
        )
        series = series.reshape(seqs, span, -1)
        return series + alter[None, :, None] * top[:, None, :] / period

    first_full, first_hat, first_inv = layer_norm(tokens.astype(jnp.float32), mixgain, mixbias)
    normed = first_full.astype(jnp.bfloat16)
    query = jnp.dot(normed, query_weight, preferred_element_type=jnp.float32)
    key = jnp.dot(normed, key_weight, preferred_element_type=jnp.float32)
    value = jnp.dot(normed, value_weight, preferred_element_type=jnp.float32)
    query3 = query.reshape(seqs, span, chans)
    key3 = key.reshape(seqs, span, chans)
    value3 = value.reshape(seqs, span, chans)
    lagged = [jnp.pad(key3, ((0, 0), (lag, 0), (0, 0)))[:, :span] for lag in range(lags)]
    shifted = sum((shift_taps[lag] * lagged[lag] for lag in range(lags)))
    signal = mask3 * shifted * value3
    sig_real, sig_imag, sig_top = forward_bins(signal)
    top_kernel = nyquist(state_coef, state_rate, span)
    spec_real, spec_imag = (
        lax.all_to_all(sig_real, "freq", split_axis=1, concat_axis=0, tiled=True),
        lax.all_to_all(sig_imag, "freq", split_axis=1, concat_axis=0, tiled=True),
    )
    bins = lax.axis_index("freq") * width + jnp.arange(width)
    ker_real, ker_imag = blocked_spectrum(state_coef, state_rate, bins, span)
    prod_real = spec_real * ker_real - spec_imag * ker_imag
    prod_imag = spec_real * ker_imag + spec_imag * ker_real
    conv_real, conv_imag = (
        lax.all_to_all(prod_real, "freq", split_axis=0, concat_axis=1, tiled=True),
        lax.all_to_all(prod_imag, "freq", split_axis=0, concat_axis=1, tiled=True),
    )
    conv = inverse_bins(conv_real, conv_imag, sig_top * top_kernel)
    mixed = conv + state_skip * signal
    gated = (mask3 * query3 * mixed).reshape(rows, chans).astype(jnp.bfloat16)
    mixout = lax.psum(jnp.dot(gated, out_weight, preferred_element_type=jnp.float32), "tp")
    resid = tokens.astype(jnp.float32) + mixout
    second_full, second_hat, second_inv = layer_norm(resid, feedgain, feedbias)
    second = second_full.astype(jnp.bfloat16)
    hidden = jnp.dot(second, up_weight, preferred_element_type=jnp.float32) + up_bias
    activated = jax.nn.gelu(hidden, approximate=False).astype(jnp.bfloat16)
    down_part = jnp.dot(activated, down_weight, preferred_element_type=jnp.float32)
    down_sum = lax.psum(down_part, "tp") + down_bias
    layer_out = (mask * (resid + down_sum)).astype(jnp.bfloat16)
    grad_out = mask * cotangent.astype(jnp.float32)
    grad_down = grad_out.astype(jnp.bfloat16)
    downweight_part = inner(activated, grad_down)
    downbias_part = jnp.sum(grad_down.astype(jnp.float32), 0)
    grad_hidden = (times_transposed(grad_down, down_weight) * gelu_slope(hidden)).astype(
        jnp.bfloat16
    )
    upweight_part = inner(second, grad_hidden)
    upbias_part = jnp.sum(grad_hidden.astype(jnp.float32), 0)
    grad_second = lax.psum(times_transposed(grad_hidden, up_weight), "tp")
    grad_resid = grad_out + norm_back(grad_second, second_hat, second_inv, feedgain)
    feedgain_part = jnp.sum(grad_second * second_hat, 0)
    feedbias_part = jnp.sum(grad_second, 0)
    grad_mix = grad_resid.astype(jnp.bfloat16)
    outweight_part = inner(gated, grad_mix)
    grad_gated = times_transposed(grad_mix, out_weight).reshape(seqs, span, chans)
    grad_query = (mask3 * grad_gated * mixed).reshape(rows, chans).astype(jnp.bfloat16)
    grad_mixed = mask3 * grad_gated * query3
    skip_part = jnp.sum(grad_mixed * signal, (0, 1))
    grad_real, grad_imag, grad_top = forward_bins(grad_mixed)
    gbin_real, gbin_imag = (
        lax.all_to_all(grad_real, "freq", split_axis=1, concat_axis=0, tiled=True),
        lax.all_to_all(grad_imag, "freq", split_axis=1, concat_axis=0, tiled=True),
    )
    back_real = ker_real * gbin_real + ker_imag * gbin_imag
    back_imag = ker_real * gbin_imag - ker_imag * gbin_real
    bin_fold = (jnp.where(bins == 0, 1.0, 2.0).astype(jnp.float32) / period)[:, None]
    cot_real = bin_fold * jnp.sum(spec_real * gbin_real + spec_imag * gbin_imag, 0)
    cot_imag = -bin_fold * jnp.sum(spec_imag * gbin_real - spec_real * gbin_imag, 0)
    coef_bins, rate_bins = spectrum_grads(state_coef, state_rate, bins, span, cot_real, cot_imag)
    corr_real, corr_imag = (
        lax.all_to_all(back_real, "freq", split_axis=0, concat_axis=1, tiled=True),
        lax.all_to_all(back_imag, "freq", split_axis=0, concat_axis=1, tiled=True),
    )
    top_cot = jnp.sum(sig_top * grad_top, 0) / period
    _, top_pull = jax.vjp(
        lambda part_coef, part_rate: nyquist(part_coef, part_rate, span), state_coef, state_rate
    )
    coef_top, rate_top = top_pull(top_cot)
    coef_part = coef_bins + coef_top
    rate_part = rate_bins + rate_top
    grad_signal = state_skip * grad_mixed + inverse_bins(
        corr_real, corr_imag, grad_top * top_kernel
    )
    grad_shifted = grad_signal * mask3 * value3
    grad_value = (grad_signal * mask3 * shifted).reshape(rows, chans).astype(jnp.bfloat16)
    grad_key3 = sum(
        (
            shift_taps[lag] * jnp.pad(grad_shifted, ((0, 0), (0, lag), (0, 0)))[:, lag:]
            for lag in range(lags)
        )
    )
    grad_key = grad_key3.reshape(rows, chans).astype(jnp.bfloat16)
    taps_part = jnp.stack([jnp.sum(grad_shifted * lagged[lag], (0, 1)) for lag in range(lags)])
    query_part = inner(normed, grad_query)
    key_part = inner(normed, grad_key)
    value_part = inner(normed, grad_value)
    local_normed = (
        times_transposed(grad_query, query_weight)
        + times_transposed(grad_key, key_weight)
        + times_transposed(grad_value, value_weight)
    )
    grad_normed = lax.psum(local_normed, "tp")
    tokens_grad = grad_resid + norm_back(grad_normed, first_hat, first_inv, mixgain)
    mixgain_part = jnp.sum(grad_normed * first_hat, 0)
    mixbias_part = jnp.sum(grad_normed, 0)
    query_sum, key_sum, value_sum, upweight_sum = (
        lax.psum_scatter(query_part, "freq", scatter_dimension=0, tiled=True),
        lax.psum_scatter(key_part, "freq", scatter_dimension=0, tiled=True),
        lax.psum_scatter(value_part, "freq", scatter_dimension=0, tiled=True),
        lax.psum_scatter(upweight_part, "freq", scatter_dimension=0, tiled=True),
    )
    outweight_sum, downweight_sum = (
        lax.psum_scatter(outweight_part, "freq", scatter_dimension=1, tiled=True),
        lax.psum_scatter(downweight_part, "freq", scatter_dimension=1, tiled=True),
    )
    totals = lax.psum(
        (
            mixgain_part,
            mixbias_part,
            taps_part,
            coef_part,
            rate_part,
            skip_part,
            feedgain_part,
            feedbias_part,
            upbias_part,
            downbias_part,
        ),
        "freq",
    )
    return (
        layer_out,
        tokens_grad,
        totals[0],
        totals[1],
        query_sum,
        key_sum,
        value_sum,
        totals[2],
        totals[3],
        totals[4],
        totals[5],
        outweight_sum,
        totals[6],
        totals[7],
        upweight_sum,
        totals[8],
        downweight_sum,
        totals[9],
    )


def solution(mesh):
    in_specs = (
        P("freq", None),
        P("freq"),
        P(),
        P(),
        P(None, "tp"),
        P(None, "tp"),
        P(None, "tp"),
        P(None, "tp"),
        P("tp", None),
        P("tp", None),
        P("tp"),
        P("tp", None),
        P(),
        P(),
        P(None, "tp"),
        P("tp"),
        P("tp", None),
        P(),
        P("freq", None),
    )
    out_specs = (
        P("freq", None),
        P("freq", None),
        P(),
        P(),
        P("freq", "tp"),
        P("freq", "tp"),
        P("freq", "tp"),
        P(None, "tp"),
        P("tp", None),
        P("tp", None),
        P("tp"),
        P("tp", "freq"),
        P(),
        P(),
        P("freq", "tp"),
        P("tp"),
        P("tp", "freq"),
        P(),
    )
    return jax.shard_map(body, mesh=mesh, in_specs=in_specs, out_specs=out_specs, check_vma=False)
```

profile of v0, /device:TPU:0, one launch (start us, length us, event | category | flops | bytes accessed | tf_op | source)
XLA Modules:
  0.0 1526.7 jit_solution(8463584590916798998)
XLA Ops:
  38.9 8.8 all-to-all-start.1
  63.2 18.6 %all-to-all-done.1 = f32[1,1024,384]{2,0,1:T(1,128)} async-done(((f32[1,1024,384]{2,0,1:T(1,128)}), f32[1,1024,384]{2,0,1:T(1,128)}, u32[]{:S(2)}, u32[]{:S(2)}) %all-to-all-start.1) | async-done | bytes 1572896 | tf_op jit(solution)/shard_map/all_to_all | solution.py:192
  97.8 25.3 %all-to-all-done = f32[1,1024,384]{2,0,1:T(1,128)} async-done(((f32[1,1024,384]{2,0,1:T(1,128)}), f32[1,1024,384]{2,0,1:T(1,128)}, u32[]{:S(2)}, u32[]{:S(2)}) %all-to-all-start) | async-done | bytes 1572896 | tf_op jit(solution)/shard_map/all_to_all | solution.py:191
  126.6 44.0 %all_to_all.84 = f32[16,64,384]{2,1,0:T(8,128)} all-to-all(f32[16,64,384]{2,1,0:T(8,128)S(1)} %get-tuple-element.106), channel_id=1, replica_groups=mesh['freq'=16,'tp'=2] {'freq'}, dimensions={0} | all-to-all | bytes 3145728 | tf_op jit(solution)/shard_map/all_to_all | solution.py:200
  181.0 27.2 %all-to-all-done.2 = f32[16,64,384]{2,1,0:T(8,128)} async-done(((f32[16,64,384]{2,1,0:T(8,128)}), f32[16,64,384]{2,1,0:T(8,128)}, u32[]{:S(2)}, u32[]{:S(2)}) %all-to-all-start.2) | async-done | bytes 1572896 | tf_op jit(solution)/shard_map/all_to_all | solution.py:199
  246.0 25.0 %all-reduce.14.cloned.1.call-done = f32[1024,768]{1,0:T(8,128)} async-done(((f32[1024,768]{1,0:T(8,128)}), f32[1024,768]{1,0:T(8,128)}) %all-reduce.14.cloned.1.call-update) | async-done | bytes 3145744 | tf_op jit(solution)/shard_map/psum | solution.py:205
  274.5 17.4 %fusion.2 = (bf16[1024,1536]{1,0:T(8,128)(2,1)}, f32[1024,1536]{1,0:T(8,128)S(1)}) fusion(f32[1536]{0:T(1024)S(1)} %copy-done.89, bf16[768,1536]{1,0:T(8,128)(2,1)S(1)} %copy-done, f32[1024,768]{1,0:T(8,128)S(1)} %get-tuple-element.101, f32[768]{0:T(1024)S(1)} %copy-done.90, f32[768]{0:T(1024)S(1)} %copy-done.76, f32[1024]{0:T(1024)S(1)} %add_rsqrt_fusion, ...), kind=kOutput, calls=%fused_computation.10 | convolution fusion | flops 2523660288 | bytes 14962688 | tf_op jit(solution)/shard_map/dot_general | solution.py:209
  302.7 24.6 %all-reduce.16.cloned.1.call-done = f32[1024,768]{1,0:T(8,128)} async-done(((f32[1024,768]{1,0:T(8,128)}), f32[1024,768]{1,0:T(8,128)}) %all-reduce.16.cloned.1.call-update) | async-done | bytes 3145744 | tf_op jit(solution)/shard_map/psum | solution.py:223
  380.1 18.7 %all-to-all-done.5 = f32[1,1024,384]{2,0,1:T(1,128)} async-done(((f32[1,1024,384]{2,0,1:T(1,128)}), f32[1,1024,384]{2,0,1:T(1,128)}, u32[]{:S(2)}, u32[]{:S(2)}) %all-to-all-start.5) | async-done | bytes 1572896 | tf_op jit(solution)/shard_map/all_to_all | solution.py:236
  398.8 8.2 all-to-all-start.4
  409.7 31.1 %all-to-all-done.4 = f32[1,1024,384]{2,0,1:T(1,128)} async-done(((f32[1,1024,384]{2,0,1:T(1,128)}), f32[1,1024,384]{2,0,1:T(1,128)}, u32[]{:S(2)}, u32[]{:S(2)}) %all-to-all-start.4) | async-done | bytes 1572896 | tf_op jit(solution)/shard_map/all_to_all | solution.py:235
  447.2 44.1 %all_to_all.85 = f32[16,64,384]{2,1,0:T(8,128)} all-to-all(f32[16,64,384]{2,1,0:T(8,128)S(1)} %get-tuple-element.108), channel_id=1, replica_groups=mesh['freq'=16,'tp'=2] {'freq'}, dimensions={0} | all-to-all | bytes 3145728 | tf_op jit(solution)/shard_map/all_to_all | solution.py:245
  506.3 22.6 %all-to-all-done.7 = f32[16,64,384]{2,1,0:T(8,128)} async-done(((f32[16,64,384]{2,1,0:T(8,128)}), f32[16,64,384]{2,1,0:T(8,128)}, u32[]{:S(2)}, u32[]{:S(2)}) %all-to-all-start.7) | async-done | bytes 1572896 | tf_op jit(solution)/shard_map/all_to_all | solution.py:246
  577.8 9.0 fusion.47
  587.7 8.1 fusion.284
  595.9 7.9 fusion.280
  613.8 78.2 %all-reduce.6 = (f32[768]{0:T(1024)}, f32[768]{0:T(1024)}, f32[4,384]{1,0:T(4,128)}, f32[384]{0:T(512)}, f32[768]{0:T(1024)}, /*index=5*/f32[768]{0:T(1024)}, f32[1536]{0:T(1024)}, f32[768]{0:T(1024)}) all-reduce(f32[768]{0:T(1024)S(1)} %get-tuple-element.64, ...), channel_id=1, replica_groups=mesh['freq'=16,'tp'=2] {'freq'}, use_global_device_ids=true, to_apply=%region_16.17 | all-reduce | flops 7296 | bytes 58368 | tf_op jit(solution)/shard_map/psum | solution.py:290
  700.1 35.4 %reduce-scatter.13.cloned.1.call-done = f32[384,48]{0,1:T(8,128)} async-done(((f32[384,768]{0,1:T(8,128)}), f32[384,48]{0,1:T(8,128)}) %reduce-scatter.13.cloned.1.call-update) | async-done | bytes 73744 | tf_op jit(solution)/shard_map/reduce_scatter | solution.py:287
  735.5 128.5 %reduce-scatter.7.cloned.1.call-done = f32[48,384]{1,0:T(8,128)} async-done(((f32[768,384]{1,0:T(8,128)}), f32[48,384]{1,0:T(8,128)}) %reduce-scatter.7.cloned.1.call-update) | async-done | bytes 73744 | tf_op jit(solution)/shard_map/reduce_scatter | solution.py:281
  864.0 112.6 %all-reduce.18.cloned.1.call-done = (f32[384,64]{0,1:T(8,128)}, f32[384,64]{0,1:T(8,128)}) async-done(((f32[384,64]{0,1:T(8,128)}, f32[384,64]{0,1:T(8,128)}), (f32[384,64]{0,1:T(8,128)}, f32[384,64]{0,1:T(8,128)})) %all-reduce.18.cloned.1.call-update) | async-done | bytes 196624 | tf_op jit(solution)/shard_map/psum | solution.py:290
  976.7 141.6 %reduce-scatter.15.cloned.1.call-done = f32[48,1536]{1,0:T(8,128)} async-done(((f32[768,1536]{1,0:T(8,128)}), f32[48,1536]{1,0:T(8,128)}) %reduce-scatter.15.cloned.1.call-update) | async-done | bytes 294928 | tf_op jit(solution)/shard_map/reduce_scatter | solution.py:284
  1118.3 142.4 %reduce-scatter.17.cloned.1.call-done = f32[1536,48]{0,1:T(8,128)} async-done(((f32[1536,768]{0,1:T(8,128)}), f32[1536,48]{0,1:T(8,128)}) %reduce-scatter.17.cloned.1.call-update) | async-done | bytes 294928 | tf_op jit(solution)/shard_map/reduce_scatter | solution.py:288
  1260.7 128.1 %reduce-scatter.11.cloned.1.call-done = f32[48,384]{1,0:T(8,128)} async-done(((f32[768,384]{1,0:T(8,128)}), f32[48,384]{1,0:T(8,128)}) %reduce-scatter.11.cloned.1.call-update) | async-done | bytes 73744 | tf_op jit(solution)/shard_map/reduce_scatter | solution.py:283
  1388.8 127.9 %reduce-scatter.9.cloned.1.call-done = f32[48,384]{1,0:T(8,128)} async-done(((f32[768,384]{1,0:T(8,128)}), f32[48,384]{1,0:T(8,128)}) %reduce-scatter.9.cloned.1.call-update) | async-done | bytes 73744 | tf_op jit(solution)/shard_map/reduce_scatter | solution.py:282
  (314 shorter events, 274.7 us)
Async XLA Ops:
  7.2 267.1 %copy-start = (bf16[768,1536]{1,0:T(8,128)(2,1)S(1)}, bf16[768,1536]{1,0:T(8,128)(2,1)}, u32[]{:S(2)}) copy-start(bf16[768,1536]{1,0:T(8,128)(2,1)} %param.33) | copy-start | bytes 7077892
  38.9 43.0 %all-to-all-start.1 = ((f32[1,1024,384]{2,0,1:T(1,128)}), f32[1,1024,384]{2,0,1:T(1,128)}, u32[]{:S(2)}, u32[]{:S(2)}) async-start(f32[1,1024,384]{2,0,1:T(1,128)} %copy.143), calls=%async_computation.1 | async-start | bytes 3145728 | tf_op jit(solution)/shard_map/all_to_all | solution.py:192
  81.8 41.3 %all-to-all-start = ((f32[1,1024,384]{2,0,1:T(1,128)}), f32[1,1024,384]{2,0,1:T(1,128)}, u32[]{:S(2)}, u32[]{:S(2)}) async-start(f32[1,1024,384]{2,0,1:T(1,128)} %copy.139), calls=%async_computation | async-start | bytes 3145728 | tf_op jit(solution)/shard_map/all_to_all | solution.py:191
  89.6 35.2 %copy-start.80 = (f32[64]{0:T(128)}, f32[64]{0:T(128)S(1)}, u32[]{:S(2)}) copy-start(f32[64]{0:T(128)S(1)} %fusion.180) | copy-start | bytes 772
  90.1 34.6 %copy-start.82 = (f32[64]{0:T(128)}, f32[64]{0:T(128)S(1)}, u32[]{:S(2)}) copy-start(f32[64]{0:T(128)S(1)} %get-tuple-element.134) | copy-start | bytes 772
  90.6 34.1 %copy-start.84 = (f32[64]{0:T(128)}, f32[64]{0:T(128)S(1)}, u32[]{:S(2)}) copy-start(f32[64]{0:T(128)S(1)} %get-tuple-element.133) | copy-start | bytes 772
  90.7 34.1 %copy-start.48 = (f32[384,64]{0,1:T(8,128)}, f32[384,64]{0,1:T(8,128)S(1)}, u32[]{:S(2)}) copy-start(f32[384,64]{0,1:T(8,128)S(1)} %get-tuple-element.117) | copy-start | bytes 294916
  90.7 34.1 %copy-start.50 = (f32[384,64]{0,1:T(8,128)}, f32[384,64]{0,1:T(8,128)S(1)}, u32[]{:S(2)}) copy-start(f32[384,64]{0,1:T(8,128)S(1)} %get-tuple-element.119) | copy-start | bytes 294916
  170.6 37.7 %all-to-all-start.2 = ((f32[16,64,384]{2,1,0:T(8,128)}), f32[16,64,384]{2,1,0:T(8,128)}, u32[]{:S(2)}, u32[]{:S(2)}) async-start(f32[16,64,384]{2,1,0:T(8,128)} %get-tuple-element.107), calls=%async_computation.2 | async-start | bytes 3145728 | tf_op jit(solution)/shard_map/all_to_all | solution.py:199
  175.1 95.9 %all-reduce.14.cloned.1.call-start = ((), (), s32[]{:S(2)}) async-start(), calls=%async_computation.14 | async-start | bytes 6291456 | tf_op jit(solution)/shard_map/psum | solution.py:205
  245.9 81.4 %all-reduce.16.cloned.1.call-start = ((), (), s32[]{:S(2)}) async-start(), calls=%async_computation.15 | async-start | bytes 6291456 | tf_op jit(solution)/shard_map/psum | solution.py:223
  357.6 41.2 %all-to-all-start.5 = ((f32[1,1024,384]{2,0,1:T(1,128)}), f32[1,1024,384]{2,0,1:T(1,128)}, u32[]{:S(2)}, u32[]{:S(2)}) async-start(f32[1,1024,384]{2,0,1:T(1,128)} %copy.160), calls=%async_computation.5 | async-start | bytes 3145728 | tf_op jit(solution)/shard_map/all_to_all | solution.py:236
  398.8 42.0 %all-to-all-start.4 = ((f32[1,1024,384]{2,0,1:T(1,128)}), f32[1,1024,384]{2,0,1:T(1,128)}, u32[]{:S(2)}, u32[]{:S(2)}) async-start(f32[1,1024,384]{2,0,1:T(1,128)} %copy.156), calls=%async_computation.4 | async-start | bytes 3145728 | tf_op jit(solution)/shard_map/all_to_all | solution.py:235
  491.4 37.5 %all-to-all-start.7 = ((f32[16,64,384]{2,1,0:T(8,128)}), f32[16,64,384]{2,1,0:T(8,128)}, u32[]{:S(2)}, u32[]{:S(2)}) async-start(f32[16,64,384]{2,1,0:T(8,128)} %get-tuple-element.109), calls=%async_computation.7 | async-start | bytes 3145728 | tf_op jit(solution)/shard_map/all_to_all | solution.py:246
  495.8 115.0 %all-reduce.20.cloned.1.call-start = ((), (), s32[]{:S(2)}) async-start(), calls=%async_computation.23 | async-start | bytes 12582912 | tf_op jit(solution)/shard_map/psum | solution.py:212
  570.9 164.7 %reduce-scatter.13.cloned.1.call-start = ((), (), s32[]{:S(2)}) async-start(), calls=%async_computation.19 | async-start | bytes 1253376 | tf_op jit(solution)/shard_map/reduce_scatter | solution.py:287
  575.1 288.9 %reduce-scatter.7.cloned.1.call-start = ((), (), s32[]{:S(2)}) async-start(), calls=%async_computation.16 | async-start | bytes 1253376 | tf_op jit(solution)/shard_map/reduce_scatter | solution.py:281
  577.4 399.2 %all-reduce.18.cloned.1.call-start = ((), (), s32[]{:S(2)}) async-start(), calls=%async_computation.22 | async-start | bytes 393216 | tf_op jit(solution)/shard_map/psum | solution.py:290
  587.6 530.7 %reduce-scatter.15.cloned.1.call-start = ((), (), s32[]{:S(2)}) async-start(), calls=%async_computation.20 | async-start | bytes 5013504 | tf_op jit(solution)/shard_map/reduce_scatter | solution.py:284
  595.8 664.9 %reduce-scatter.17.cloned.1.call-start = ((), (), s32[]{:S(2)}) async-start(), calls=%async_computation.21 | async-start | bytes 5013504 | tf_op jit(solution)/shard_map/reduce_scatter | solution.py:288
  603.8 785.0 %reduce-scatter.11.cloned.1.call-start = ((), (), s32[]{:S(2)}) async-start(), calls=%async_computation.18 | async-start | bytes 1253376 | tf_op jit(solution)/shard_map/reduce_scatter | solution.py:283
  607.0 909.6 %reduce-scatter.9.cloned.1.call-start = ((), (), s32[]{:S(2)}) async-start(), calls=%async_computation.17 | async-start | bytes 1253376 | tf_op jit(solution)/shard_map/reduce_scatter | solution.py:282
  610.6 81.4 %copy-start.79 = (f32[768]{0:T(1024)S(1)}, f32[768]{0:T(1024)}, u32[]{:S(2)}) copy-start(f32[768]{0:T(1024)} %param.36) | copy-start | bytes 9220
  692.0 827.7 %copy-start.1 = (bf16[768,1536]{1,0:T(8,128)(2,1)S(1)}, bf16[768,1536]{1,0:T(8,128)(2,1)}, u32[]{:S(2)}) copy-start(bf16[768,1536]{1,0:T(8,128)(2,1)} %param.33) | copy-start | bytes 7077892
  (84 other events, 465.4 us)
Sparse Core Ops, SparseCore 0:
  246.0 24.8 all-reduce.13
  302.8 24.4 all-reduce.15
  571.0 33.7 all-reduce.19
  610.7 124.8 reduce-scatter.12
  741.4 122.5 reduce-scatter.6
  870.6 105.9 all-reduce.17
  982.4 135.8 reduce-scatter.14
  1124.9 135.7 reduce-scatter.16
  1266.0 122.6 reduce-scatter.10
  1393.9 122.6 reduce-scatter.8
where the time goes:
time: 1540 us; the launch traced here: 1530 us
  waiting for transfers between devices  1010 us (66%)
  matrix products  202 us (13%)
  blocking collectives  166 us (11%)
  other arithmetic  52.3 us (3%)
  starting transfers between devices  41 us (3%)
  local copies, waits for them, and re-layouts  38.2 us (2%)
  between operations  16.8 us (1%)
    reduce_scatter x1, waiting for transfers between devices, body(): lax.psum_scatter(downweight_part, 'freq', scatter_dimension=1, tiled=True)  142 us
    reduce_scatter x1, waiting for transfers between devices, body(): lax.psum_scatter(upweight_part, 'freq', scatter_dimension=0, tiled=True)  142 us
    reduce_scatter x1, waiting for transfers between devices, body(): lax.psum_scatter(query_part, 'freq', scatter_dimension=0, tiled=True)  129 us
    reduce_scatter x1, waiting for transfers between devices, body(): lax.psum_scatter(value_part, 'freq', scatter_dimension=0, tiled=True)  128 us
    reduce_scatter x1, waiting for transfers between devices, body(): lax.psum_scatter(key_part, 'freq', scatter_dimension=0, tiled=True)  128 us
    psum x1, waiting for transfers between devices, body(): lax.psum((mixgain_part, mixbias_part, taps_part, coef_part, rate_part, sk...  113 us
    psum x1, blocking collectives, body(): lax.psum((mixgain_part, mixbias_part, taps_part, coef_part, rate_part, sk...  78.2 us
    all_to_all x1, blocking collectives, body(): lax.all_to_all(back_real, 'freq', split_axis=0, concat_axis=1, tiled=True)  44.1 us
  transfers between devices with their start and end apart: 16, of which 15 were waited for; matrix products, arithmetic and copies ran while one was open for 7% of the time, Pallas kernels for 0%

commit v1 on v0

v1 whole, which is shorter than its diff:
```python
import math

import jax
import jax.numpy as jnp
import numpy as np
from jax import lax
from jax.experimental import pallas as pl
from jax.experimental.pallas import tpu as pltpu
from jax.sharding import PartitionSpec as P

f32 = jnp.float32
bf16 = jnp.bfloat16


def layer_norm(value, gain, bias):
    mean = jnp.mean(value, -1, keepdims=True)
    centered = value - mean
    inverse = lax.rsqrt(jnp.mean(centered * centered, -1, keepdims=True) + 1e-05)
    scaled = centered * inverse
    return (scaled * gain + bias, scaled, inverse)


def norm_back(grad_out, scaled, inverse, gain):
    weighted = grad_out * gain
    return inverse * (
        weighted
        - jnp.mean(weighted, -1, keepdims=True)
        - scaled * jnp.mean(weighted * scaled, -1, keepdims=True)
    )


def inner(left, right):
    return lax.dot_general(left, right, (((0,), (0,)), ((), ())), preferred_element_type=f32)


def times_transposed(grad, weight):
    return lax.dot_general(grad, weight, (((1,), (1,)), ((), ())), preferred_element_type=f32)


def matmul(left, right):
    return jnp.dot(left, right, preferred_element_type=f32)


def dft_table(span):
    bins = np.arange(span)[:, None].astype(np.int64)
    times = np.arange(span)[None, :].astype(np.int64)
    angle = (bins * times % (2 * span)) * (math.pi / span)
    table = np.concatenate([np.cos(angle), np.sin(angle)], 0)
    table[span] = 1 - 2 * (np.arange(span) % 2)
    return table


def packed_product(left, right, first, sign):
    half = left.shape[0] // 2
    a, b, c, d = left[:half], left[half:], right[:half], right[half:]
    bd = b * d
    real = a * c - sign * jnp.where(first, 0.0, bd)
    imag = jnp.where(first, bd, b * c + sign * (a * d))
    return jnp.concatenate([real, imag], 0)


def swap(value, axis, bit):
    size = lax.axis_size(axis)
    return lax.ppermute(value, axis, [(i, i ^ (1 << bit)) for i in range(size)])


def pair_sum(value):
    if lax.axis_size("tp") == 1:
        return value
    return value + swap(value, "tp", 0)


def scatter_sum(value, order, after=()):
    places = lax.axis_size("freq")
    count = places.bit_length() - 1
    place = lax.axis_index("freq")
    value = value.reshape((2,) * count + (value.shape[0] // places, value.shape[1]))
    dims = list(range(count - 1, -1, -1))
    for step, bit in enumerate(order):
        dim = dims.index(bit)
        mine = (place >> bit) & 1
        give = lax.dynamic_index_in_dim(value, 1 - mine, dim, keepdims=False)
        keep = lax.dynamic_index_in_dim(value, mine, dim, keepdims=False)
        got = swap(give, "freq", bit)
        if step < len(after):
            got, _ = lax.optimization_barrier((got, after[step]))
        value = keep + got
        dims.pop(dim)
    return value


def lane_parts(chans):
    return 128 if chans % 128 == 0 else chans


def state_kernel(coef_t, rate_t, span):
    states, chans = coef_t.shape
    step = 32
    blocks = span // step
    lanes = lane_parts(chans)
    group = 8

    def run(coef_ref, rate_ref, out_ref, fine, coarse):
        rate = rate_ref[...][:, None, :]
        within = lax.broadcasted_iota(jnp.int32, (1, step, 1), 1).astype(f32)
        across = lax.broadcasted_iota(jnp.int32, (1, blocks, 1), 1).astype(f32)
        fine[...] = jnp.exp(-rate * within)
        coarse[...] = coef_ref[...][:, None, :] * jnp.exp(-rate * (step * across))
        for base in range(0, blocks, group):

            def add(n, sums):
                near = fine[n]
                return tuple(
                    sums[j] + coarse[n, pl.ds(base + j, 1), :] * near for j in range(group)
                )

            zero = jnp.zeros((step, lanes), f32)
            sums = lax.fori_loop(0, states, add, (zero,) * group, unroll=8)
            for j in range(group):
                out_ref[pl.ds((base + j) * step, step), :] = sums[j].astype(bf16)

    return pl.pallas_call(
        run,
        grid=(chans // lanes,),
        in_specs=[pl.BlockSpec((states, lanes), lambda i: (0, i))] * 2,
        out_specs=pl.BlockSpec((span, lanes), lambda i: (0, i)),
        out_shape=jax.ShapeDtypeStruct((span, chans), bf16),
        scratch_shapes=[
            pltpu.VMEM((states, step, lanes), f32),
            pltpu.VMEM((states, blocks, lanes), f32),
        ],
        compiler_params=pltpu.CompilerParams(vmem_limit_bytes=32 << 20),
        cost_estimate=pl.CostEstimate(
            flops=2 * span * chans * states, bytes_accessed=2 * span * chans, transcendentals=0
        ),
        name="state_kernel",
    )(coef_t, rate_t)


def state_grads(coef_t, rate_t, lag_grad):
    states, chans = coef_t.shape
    span = lag_grad.shape[0]
    step = 32
    blocks = span // step
    lanes = lane_parts(chans)
    group = 8
    tiles = step // 8

    def run(coef_ref, rate_ref, lag_ref, coef_out, rate_out, fine, coarse, plain, place, ramp):
        rate = rate_ref[...][:, None, :]
        within = lax.broadcasted_iota(jnp.int32, (1, step, 1), 1).astype(f32)
        across = lax.broadcasted_iota(jnp.int32, (1, blocks, 1), 1).astype(f32)
        fine[...] = jnp.exp(-rate * within)
        coarse[...] = jnp.exp(-rate * (step * across))
        plain[...] = jnp.zeros_like(plain)
        place[...] = jnp.zeros_like(place)
        ramp[...] = jnp.zeros_like(ramp)
        for base in range(0, blocks, group):
            lag = [
                [
                    lag_ref[pl.ds((base + j) * step + 8 * a, 8), :]
                    for a in range(tiles)
                ]
                for j in range(group)
            ]

            def add(n, _):
                near = [fine[n, pl.ds(8 * a, 8), :] for a in range(tiles)]
                suffix = None
                later = None
                tilted = None
                for j in reversed(range(group)):
                    far = coarse[n, pl.ds(base + j, 1), :]
                    total = None
                    slope = None
                    for a in reversed(range(tiles)):
                        term = lag[j][a] * near[a]
                        if total is None:
                            total = term
                        else:
                            slope = total if slope is None else slope + total
                            total = total + term
                    weighted = far * total
                    bent = far * slope
                    tilted = bent if tilted is None else tilted + bent
                    if suffix is None:
                        suffix = weighted
                    else:
                        later = suffix if later is None else later + suffix
                        suffix = suffix + weighted
                plain[n] = plain[n] + suffix
                place[n] = place[n] + (later + float(base) * suffix)
                ramp[n] = ramp[n] + tilted
                return 0

            lax.fori_loop(0, states, add, 0, unroll=4)
        rows = lax.broadcasted_iota(jnp.int32, (1, 8, 1), 1).astype(f32)
        whole = plain[...]
        coef_out[...] = jnp.sum(whole, 1)
        times = float(step) * place[...] + 8.0 * ramp[...] + rows * whole
        rate_out[...] = -coef_ref[...] * jnp.sum(times, 1)

    shape = jax.ShapeDtypeStruct((states, chans), f32)
    block = pl.BlockSpec((states, lanes), lambda i: (0, i))
    return pl.pallas_call(
        run,
        grid=(chans // lanes,),
        in_specs=[block, block, pl.BlockSpec((span, lanes), lambda i: (0, i))],
        out_specs=[block, block],
        out_shape=[shape, shape],
        scratch_shapes=[
            pltpu.VMEM((states, step, lanes), f32),
            pltpu.VMEM((states, blocks, lanes), f32),
        ]
        + [pltpu.VMEM((states, 8, lanes), f32)] * 3,
        compiler_params=pltpu.CompilerParams(vmem_limit_bytes=32 << 20),
        cost_estimate=pl.CostEstimate(
            flops=4 * span * chans * states, bytes_accessed=4 * span * chans, transcendentals=0
        ),
        name="state_grads",
    )(coef_t, rate_t, lag_grad)


def body(
    tokens,
    lengths,
    mixgain,
    mixbias,
    query_weight,
    key_weight,
    value_weight,
    shift_taps,
    state_coef,
    state_rate,
    state_skip,
    out_weight,
    feedgain,
    feedbias,
    up_weight,
    up_bias,
    down_weight,
    down_bias,
    cotangent,
):
    seqs = lengths.shape[0]
    rows = tokens.shape[0]
    span = rows // seqs
    assert seqs == 1
    chans = query_weight.shape[1]
    lags = shift_taps.shape[0]
    places = lax.axis_size("freq")
    count = places.bit_length() - 1
    assert places == 1 << count
    bits = list(range(count))
    orders = [bits, [1, 0] + bits[2:], [2, 0, 1] + bits[3:]]
    positions = jnp.arange(span)
    mask = (positions < lengths[0]).astype(f32)[:, None]
    table_np = dft_table(span)
    table = jnp.asarray(table_np.astype(jnp.bfloat16))
    fold = jnp.full((2 * span, 1), 1.0 / span, f32).at[0].set(0.5 / span).at[span].set(0.5 / span)
    first = (jnp.arange(span) == 0)[:, None]

    def to_bins(series):
        return matmul(table, series.astype(bf16))

    def from_bins(bins):
        return inner(table, (bins * fold).astype(bf16))

    coef_t, rate_t = state_coef.T, state_rate.T
    ker_bins = to_bins(state_kernel(coef_t, rate_t, span))

    first_full, first_hat, first_inv = layer_norm(tokens.astype(f32), mixgain, mixbias)
    normed = first_full.astype(bf16)
    query = matmul(normed, query_weight)
    key = matmul(normed, key_weight)
    value = matmul(normed, value_weight)
    lagged = [jnp.pad(key, ((lag, 0), (0, 0)))[:span] for lag in range(lags)]
    shifted = sum((shift_taps[lag] * lagged[lag] for lag in range(lags)))
    signal = mask * shifted * value
    sig_bins = to_bins(signal)
    conv = from_bins(packed_product(sig_bins, ker_bins, first, 1.0))
    mixed = conv + state_skip * signal
    gated = (mask * query * mixed).astype(bf16)
    mixout = pair_sum(matmul(gated, out_weight))
    resid = tokens.astype(f32) + mixout
    second_full, second_hat, second_inv = layer_norm(resid, feedgain, feedbias)
    second = second_full.astype(bf16)
    hidden = matmul(second, up_weight) + up_bias
    cdf = 0.5 * (1.0 + lax.erf(hidden * (1.0 / math.sqrt(2.0))))
    slope = cdf + hidden * jnp.exp(-0.5 * hidden * hidden) * (1.0 / math.sqrt(2.0 * math.pi))
    activated = (hidden * cdf).astype(bf16)
    grad_out = mask * cotangent.astype(f32)
    grad_down = grad_out.astype(bf16)
    down_grad = inner(grad_down, activated)
    third = down_grad.shape[1] // 3
    downbias_part = jnp.sum(grad_down.astype(f32), 0)
    grad_hidden = (times_transposed(grad_down, down_weight) * slope).astype(bf16)
    up_grad = inner(second, grad_hidden)
    upbias_part = jnp.sum(grad_hidden.astype(f32), 0)
    second_part = times_transposed(grad_hidden, up_weight)
    feedgain_part = jnp.sum(second_part * second_hat, 0)
    feedbias_part = jnp.sum(second_part, 0)
    grad_second = pair_sum(second_part)
    grad_resid = grad_out + norm_back(grad_second, second_hat, second_inv, feedgain)
    grad_mix = grad_resid.astype(bf16)
    out_grad = inner(grad_mix, gated)
    grad_gated = times_transposed(grad_mix, out_weight)
    grad_query = (mask * grad_gated * mixed).astype(bf16)
    query_grad = inner(normed, grad_query)
    grad_mixed = mask * grad_gated * query
    skip_part = jnp.sum(grad_mixed * signal, 0)
    grad_bins = to_bins(grad_mixed)
    grad_signal = state_skip * grad_mixed + from_bins(
        packed_product(grad_bins, ker_bins, first, -1.0)
    )
    lag_grad = from_bins(packed_product(grad_bins, sig_bins, first, -1.0))
    grad_shifted = grad_signal * mask * value
    grad_value = (grad_signal * mask * shifted).astype(bf16)
    grad_key = sum(
        (
            shift_taps[lag] * jnp.pad(grad_shifted, ((0, lag), (0, 0)))[lag:]
            for lag in range(lags)
        )
    ).astype(bf16)
    key_grad = inner(normed, grad_key)
    value_grad = inner(normed, grad_value)
    taps_part = jnp.stack([jnp.sum(grad_shifted * lagged[lag], 0) for lag in range(lags)])
    normed_part = (
        times_transposed(grad_query, query_weight)
        + times_transposed(grad_key, key_weight)
        + times_transposed(grad_value, value_weight)
    )
    mixgain_part = jnp.sum(normed_part * first_hat, 0)
    mixbias_part = jnp.sum(normed_part, 0)
    grad_normed = pair_sum(normed_part)
    tokens_grad = grad_resid + norm_back(grad_normed, first_hat, first_inv, mixgain)

    coef_part, rate_part = state_grads(coef_t, rate_t, lag_grad)

    down_sums = [
        scatter_sum(down_grad[:, i * third : (i + 1) * third], orders[i], (grad_gated, lag_grad, grad_key, normed_part)) for i in range(3)
    ]
    up_sums = [scatter_sum(up_grad[:, i * third : (i + 1) * third], orders[i], (lag_grad, grad_key, normed_part)) for i in range(3)]
    out_sum = scatter_sum(out_grad, orders[0], (grad_key,))
    query_sum = scatter_sum(query_grad, orders[1], (normed_part,))
    key_sum = scatter_sum(key_grad, orders[2])
    part = chans // 3
    value_sums = [
        scatter_sum(value_grad[:, i * part : (i + 1) * part], orders[i]) for i in range(3)
    ]

    both = jnp.stack([mixgain_part, mixbias_part, feedgain_part, feedbias_part])
    both = pair_sum(both)
    small = jnp.concatenate(
        [
            jnp.concatenate([coef_part, rate_part], 0).reshape(-1),
            taps_part.reshape(-1),
            skip_part,
            upbias_part,
            downbias_part,
            both.reshape(-1),
        ]
    ).reshape(-1, 128)
    for bit in bits:
        small = small + swap(small, "freq", bit)
    small = small.reshape(-1)
    cuts = np.cumsum(
        [
            coef_part.size,
            rate_part.size,
            taps_part.size,
            chans,
            upbias_part.size,
            downbias_part.size,
        ]
    )
    coef_sum, rate_sum, taps_sum, skip_sum, upbias_sum, downbias_sum, norms = jnp.split(small, cuts)
    norms = norms.reshape(4, -1)

    down_sum = pair_sum(matmul(activated, down_weight)) + down_bias
    layer_out = (mask * (resid + down_sum)).astype(bf16)
    return (
        layer_out,
        tokens_grad,
        norms[0],
        norms[1],
        query_sum,
        key_sum,
        jnp.concatenate(value_sums, 1),
        taps_sum.reshape(lags, chans),
        coef_sum.reshape(-1, chans).T,
        rate_sum.reshape(-1, chans).T,
        skip_sum,
        out_sum.T,
        norms[2],
        norms[3],
        jnp.concatenate(up_sums, 1),
        upbias_sum,
        jnp.concatenate(down_sums, 1).T,
        downbias_sum,
    )


def solution(mesh):
    in_specs = (
        P("freq", None),
        P("freq"),
        P(),
        P(),
        P(None, "tp"),
        P(None, "tp"),
        P(None, "tp"),
        P(None, "tp"),
        P("tp", None),
        P("tp", None),
        P("tp"),
        P("tp", None),
        P(),
        P(),
        P(None, "tp"),
        P("tp"),
        P("tp", None),
        P(),
        P("freq", None),
    )
    out_specs = (
        P("freq", None),
        P("freq", None),
        P(),
        P(),
        P("freq", "tp"),
        P("freq", "tp"),
        P("freq", "tp"),
        P(None, "tp"),
        P("tp", None),
        P("tp", None),
        P("tp"),
        P("tp", "freq"),
        P(),
        P(),
        P("freq", "tp"),
        P("tp"),
        P("tp", "freq"),
        P(),
    )
    return jax.shard_map(body, mesh=mesh, in_specs=in_specs, out_specs=out_specs, check_vma=False)
```

time: 1540 us -> 342 us (0.22)
  waiting for transfers between devices: 1010 us -> 90.5 us
  blocking collectives: 166 us -> 0 us
  matrix products: 202 us -> 65.5 us
  starting transfers between devices: 41 us -> 66.6 us
  Pallas kernels: 0 us -> 23.5 us
    reduce_scatter x6 -> x0, waiting for transfers between devices: 704 us -> none  [the longest x1 142 us: body(): lax.psum_scatter(downweight_part, 'freq', scatter_dimension=1, tiled=True)]
    psum x4 -> x0, waiting for transfers between devices: 162 us -> none  [the longest x1 113 us: body(): lax.psum((mixgain_part, mixbias_part, taps_part, coef_part, rate_part, sk...]
    all_to_all x6 -> x0, waiting for transfers between devices: 144 us -> none  [the longest x1 31.1 us: body(): lax.all_to_all(grad_real, 'freq', split_axis=1, concat_axis=0, tiled=True)]
    dot_general x32 -> x9, matrix products: 158 us -> 25.2 us  [matmul(): return jnp.dot(left, right, preferred_element_type=f32)]
    ppermute x0 -> x57, waiting for transfers between devices: none -> 90.5 us  [swap(): return lax.ppermute(value, axis, [(i, i ^ 1 << bit) for i in range(size)])]
    all_to_all x2 -> x0, blocking collectives: 88.1 us -> none  [the longest x1 44.1 us: body(): lax.all_to_all(back_real, 'freq', split_axis=0, concat_axis=1, tiled=True)]
    psum x1 -> x0, blocking collectives: 78.2 us -> none  [body(): lax.psum((mixgain_part, mixbias_part, taps_part, coef_part, rate_part, sk...]
    ppermute x0 -> x57, starting transfers between devices: none -> 66.6 us  [swap(): return lax.ppermute(value, axis, [(i, i ^ 1 << bit) for i in range(size)])]
  transfers between devices with their start and end apart: 16 -> 57, of which waited for: 15 -> 28; matrix products, arithmetic and copies ran while one was open for 7% -> 29% of each run, Pallas kernels for 0% -> 4%
where the time goes in v1:
time: 342 us; the launch traced here: 336 us
  waiting for transfers between devices  90.5 us (26%)
  starting transfers between devices  66.6 us (19%)
  matrix products  65.5 us (19%)
  local copies, waits for them, and re-layouts  45.8 us (13%)
  other arithmetic  41.2 us (12%)
  Pallas kernels  23.5 us (7%)
    ppermute x57, waiting for transfers between devices, swap(): return lax.ppermute(value, axis, [(i, i ^ 1 << bit) for i in range(size)])  90.5 us
    ppermute x57, starting transfers between devices, swap(): return lax.ppermute(value, axis, [(i, i ^ 1 << bit) for i in range(size)])  66.6 us
    dot_general x9, matrix products, matmul(): return jnp.dot(left, right, preferred_element_type=f32)  25.2 us
    dot_general x6, matrix products, times_transposed(): lax.dot_general(grad, weight, (((1,), (1,)), ((), ())), preferred_element...  21.6 us
    dot_general x9, matrix products, inner(): lax.dot_general(left, right, (((0,), (0,)), ((), ())), preferred_element_...  18.8 us
    unnamed x171, local copies, waits for them, and re-layouts  16.5 us
    pallas_call x1, Pallas kernels, state_grads(): pl.pallas_call(run, grid=(chans // lanes,), in_specs=[block, block, pl.Bl...  14.6 us
    add x47, other arithmetic, scatter_sum(): value = keep + got  14 us
  transfers between devices with their start and end apart: 57, of which 28 were waited for; matrix products, arithmetic and copies ran while one was open for 29% of the time, Pallas kernels for 4%

profile of v1, /device:TPU:0, one launch (start us, length us, event | category | flops | bytes accessed | tf_op | source)
XLA Modules:
  0.0 336.3 jit_solution(13206837686115975343)
XLA Ops:
  14.1 8.9 %state_kernel.1 = bf16[1024,384]{1,0:T(8,128)(2,1)S(1)} custom-call(f32[64,384]{1,0:T(8,128)S(1)} %bitcast.283, f32[64,384]{1,0:T(8,128)S(1)} %bitcast.285), custom_call_target="tpu_custom_call" | custom-call | flops 50331648 | bytes 786432 | tf_op jit(solution)/shard_map/state_kernel/pallas_call | solution.py:122
  28.3 3.7 %multiply_convert_fusion.4 = (bf16[1024,384]{1,0:T(8,128)(2,1)S(1)}, f32[1024,384]{1,0:T(8,128)}) fusion(f32[1024,384]{1,0:T(8,128)S(1)} %fusion.67, f32[1024]{0:T(1024)S(1)} %fusion.53, f32[1024,384]{1,0:T(8,128)S(1)} %get-tuple-element.152, f32[384]{0:T(512)S(1)} %copy-done.70, bf16[2048,1024]{1,0:T(8,128)(2,1)S(1)} %copy-done.71, ...), kind=kOutput, calls=%fused_computation.71 | convolution fusion | flops 1614938112 | bytes 12858880 | tf_op jit(solution)/shard_map/dot_general | solution.py:33
  41.6 4.2 %fusion.61 = (f32[1024]{0:T(1024)S(1)}, f32[1024,768]{0,1:T(8,128)S(1)}) fusion(f32[1024,768]{0,1:T(8,128)} %fusion.70, f32[1024,768]{0,1:T(8,128)} %collective-permute-done, bf16[1024,768]{0,1:T(8,128)(2,1)} %copy.50), kind=kLoop, calls=%fused_computation.256 | loop fusion | flops 3144704 | bytes 11014144 | tf_op jit(solution)/shard_map/reduce_sum | solution.py:16
  46.6 5.5 %multiply_convert_fusion = (bf16[1024,1536]{1,0:T(8,128)(2,1)}, f32[1024,1536]{1,0:T(8,128)S(1)}) fusion(f32[1536]{0:T(1024)S(1)} %copy-done.68, bf16[768,1536]{1,0:T(8,128)(2,1)S(1)} %copy-done, f32[1024,768]{0,1:T(8,128)S(1)} %get-tuple-element.151, f32[768]{0:T(1024)S(1)} %copy-done.69, f32[768]{0:T(1024)S(1)} %copy-done.64, f32[1024]{0:T(1024)S(1)} %add_rsqrt_fusion, ...), kind=kOutput, calls=%fused_computation.8 | convolution fusion | flops 2429288448 | bytes 14962688 | tf_op jit(solution)/shard_map/dot_general | solution.py:41
  52.1 5.7 %convert_reduce_fusion = (f32[1536]{0:T(1024)}, bf16[1024,1536]{1,0:T(8,128)(2,1)S(1)}) fusion(f32[1024,1536]{1,0:T(8,128)S(1)} %get-tuple-element.213, f32[1536]{0:T(1024)S(1)} %copy-done.68, bf16[1536,768]{1,0:T(8,128)(2,1)S(1)} %copy-done.66, bf16[1024,768]{0,1:T(8,128)(2,1)S(1)} %copy-done.15, f32[1024]{0:T(1024)S(1)} %fusion.53), kind=kOutput, calls=%fused_computation.7 | convolution fusion | flops 2438724096 | bytes 13385728 | tf_op jit(solution)/shard_map/dot_general | solution.py:37
  57.8 4.3 %fusion.66 = (f32[768]{0:T(1024)S(1)}, f32[1024,768]{1,0:T(8,128)}) fusion(bf16[1024,1536]{1,0:T(8,128)(2,1)S(1)} %get-tuple-element.216, bf16[768,1536]{1,0:T(8,128)(2,1)S(1)} %copy-done), kind=kOutput, calls=%fused_computation.261 | convolution fusion | flops 2416704768 | bytes 8653824 | tf_op jit(solution)/shard_map/dot_general | solution.py:37
  62.1 3.8 %copy.55 = f32[1024,768]{0,1:T(8,128)} copy(f32[1024,768]{1,0:T(8,128)} %get-tuple-element.218) | data formatting | bytes 6291456 | tf_op jit(solution)/shard_map/dot_general | solution.py:37
  66.3 4.8 %fusion.71 = f32[1024,768]{0,1:T(8,128)S(1)} fusion(bf16[1024,1536]{1,0:T(8,128)(2,1)} %get-tuple-element.212, bf16[1536,768]{1,0:T(8,128)(2,1)S(1)} %copy-done.67), kind=kOutput, calls=%fused_computation.266 | convolution fusion | flops 2415919104 | bytes 8650752 | tf_op jit(solution)/shard_map/dot_general | solution.py:41
  94.9 3.7 %multiply_add_fusion = (f32[1024,768]{0,1:T(8,128)S(1)}, bf16[1024,768]{0,1:T(8,128)(2,1)}, f32[768]{0:T(1024)}) fusion(f32[1024,768]{0,1:T(8,128)S(1)} %get-tuple-element.149, bf16[1024,768]{0,1:T(8,128)(2,1)S(1)} %copy-done.16, f32[1024,768]{0,1:T(8,128)S(1)} %copy-done.8, f32[1024]{0:T(1024)S(1)} %get-tuple-element.219, f32[1024]{0:T(1024)S(1)} %get-tuple-element.220, ...), kind=kLoop, calls=%fused_computation.37 | loop fusion | flops 13368576 | bytes 18900992 | tf_op jit(solution)/shard_map/add | solution.py:304
  126.9 14.6 %state_grads.1 = (f32[64,384]{1,0:T(8,128)S(1)}, f32[64,384]{1,0:T(8,128)S(1)}) custom-call(f32[64,384]{1,0:T(8,128)S(1)} %bitcast.284, f32[64,384]{1,0:T(8,128)S(1)} %bitcast.286, f32[1024,384]{1,0:T(8,128)S(1)} %fusion.31.lag_ref), custom_call_target="tpu_custom_call" | custom-call | flops 100663296 | bytes 1572864 | tf_op jit(solution)/shard_map/state_grads/pallas_call | solution.py:205
  166.9 4.4 %add_add_fusion = f32[1024,768]{0,1:T(8,128)S(1)} fusion(f32[1024,768]{0,1:T(8,128)} %fusion.72, f32[1024,768]{0,1:T(8,128)} %fusion.73, bf16[1024,384]{1,0:T(8,128)(2,1)} %copy-done.45, bf16[768,384]{1,0:T(8,128)(2,1)} %param.30), kind=kOutput, calls=%fused_computation.36 | convolution fusion | flops 605552640 | bytes 10813440 | tf_op jit(solution)/shard_map/dot_general | solution.py:37
  178.5 5.1 %collective-permute-done.25 = f32[2,2,2,48,128]{4,3,1,0,2:T(8,128)S(1)} collective-permute-done((f32[2,2,2,48,128]{4,3,1,0,2:T(8,128)S(1)}, f32[2,2,2,48,128]{4,3,1,0,2:T(8,128)S(1)}, u32[]{:S(2)}, u32[]{:S(2)}) %collective-permute-start.25) | collective-permute-done | bytes 196640 | tf_op jit(solution)/shard_map/ppermute | solution.py:64
  189.1 3.7 %collective-permute-done.22 = f32[2,2,48,128]{3,2,1,0:T(8,128)S(1)} collective-permute-done((f32[2,2,48,128]{3,2,1,0:T(8,128)S(1)}, f32[2,2,48,128]{3,2,1,0:T(8,128)S(1)}, u32[]{:S(2)}, u32[]{:S(2)}) %collective-permute-start.22) | collective-permute-done | bytes 98336 | tf_op jit(solution)/shard_map/ppermute | solution.py:64
  193.7 3.7 %collective-permute-done.26 = f32[2,2,48,128]{3,2,1,0:T(8,128)S(1)} collective-permute-done((f32[2,2,48,128]{3,2,1,0:T(8,128)S(1)}, f32[2,2,48,128]{3,2,1,0:T(8,128)S(1)}, u32[]{:S(2)}, u32[]{:S(2)}) %collective-permute-start.26) | collective-permute-done | bytes 98336 | tf_op jit(solution)/shard_map/ppermute | solution.py:64
  202.0 3.9 %collective-permute-done.23 = f32[2,48,128]{2,1,0:T(8,128)S(1)} collective-permute-done((f32[2,48,128]{2,1,0:T(8,128)S(1)}, f32[2,48,128]{2,1,0:T(8,128)S(1)}, u32[]{:S(2)}, u32[]{:S(2)}) %collective-permute-start.23) | collective-permute-done | bytes 49184 | tf_op jit(solution)/shard_map/ppermute | solution.py:64
  237.9 4.5 %collective-permute-done.47 = f32[2,48,512]{2,1,0:T(8,128)S(1)} collective-permute-done((f32[2,48,512]{2,1,0:T(8,128)S(1)}, f32[2,48,512]{2,1,0:T(8,128)S(1)}, u32[]{:S(2)}, u32[]{:S(2)}) %collective-permute-start.47) | collective-permute-done | bytes 196640 | tf_op jit(solution)/shard_map/ppermute | solution.py:64
  257.5 6.3 %collective-permute-done.9 = f32[2,2,2,48,384]{4,3,1,0,2:T(8,128)S(1)} collective-permute-done((f32[2,2,2,48,384]{4,3,1,0,2:T(8,128)S(1)}, f32[2,2,2,48,384]{4,3,1,0,2:T(8,128)S(1)}, u32[]{:S(2)}, u32[]{:S(2)}) %collective-permute-start.9) | collective-permute-done | bytes 589856 | tf_op jit(solution)/shard_map/ppermute | solution.py:64
  271.7 4.0 %collective-permute-done.36 = f32[48,512]{1,0:T(8,128)S(1)} collective-permute-done((f32[48,512]{1,0:T(8,128)S(1)}, f32[48,512]{1,0:T(8,128)S(1)}, u32[]{:S(2)}, u32[]{:S(2)}) %collective-permute-start.36) | collective-permute-done | bytes 98336 | tf_op jit(solution)/shard_map/ppermute | solution.py:64
  279.5 4.3 %collective-permute-done.14 = f32[2,2,48,384]{3,2,1,0:T(8,128)S(1)} collective-permute-done((f32[2,2,48,384]{3,2,1,0:T(8,128)S(1)}, f32[2,2,48,384]{3,2,1,0:T(8,128)S(1)}, u32[]{:S(2)}, u32[]{:S(2)}) %collective-permute-start.14) | collective-permute-done | bytes 294944 | tf_op jit(solution)/shard_map/ppermute | solution.py:64
  300.9 5.9 %collective-permute-done.5 = f32[441,128]{1,0:T(8,128)S(1)} collective-permute-done((f32[441,128]{1,0:T(8,128)S(1)}, f32[441,128]{1,0:T(8,128)S(1)}, u32[]{:S(2)}, u32[]{:S(2)}) %collective-permute-start.5) | collective-permute-done | bytes 225824 | tf_op jit(solution)/shard_map/ppermute | solution.py:64
  308.5 5.2 %collective-permute-done.6 = f32[441,128]{1,0:T(8,128)S(1)} collective-permute-done((f32[441,128]{1,0:T(8,128)S(1)}, f32[441,128]{1,0:T(8,128)S(1)}, u32[]{:S(2)}, u32[]{:S(2)}) %collective-permute-start.6) | collective-permute-done | bytes 225824 | tf_op jit(solution)/shard_map/ppermute | solution.py:64
  315.9 4.2 %collective-permute-done.7 = f32[441,128]{1,0:T(8,128)S(1)} collective-permute-done((f32[441,128]{1,0:T(8,128)S(1)}, f32[441,128]{1,0:T(8,128)S(1)}, u32[]{:S(2)}, u32[]{:S(2)}) %collective-permute-start.7) | collective-permute-done | bytes 225824 | tf_op jit(solution)/shard_map/ppermute | solution.py:64
  322.8 5.7 %fusion.17 = f32[1024,768]{0,1:T(8,128)} fusion(f32[1024,768]{0,1:T(8,128)} %copy-done.6, bf16[1024,768]{0,1:T(8,128)(2,1)S(1)} %copy-done.5, f32[1024,768]{0,1:T(8,128)} %get-tuple-element.148, f32[1024]{0:T(1024)S(1)} %broadcast_multiply_fusion, f32[1024]{0:T(1024)S(1)} %broadcast_multiply_fusion.1, f32[1024]{0:T(1024)S(1)} %add_rsqrt_fusion.1, ...), kind=kLoop, calls=%fused_computation.24 | loop fusion | flops 6291456 | bytes 11026432 | tf_op jit(solution)/shard_map/add | solution.py:336
  328.5 3.7 %copy.85 = f32[1024,768]{1,0:T(8,128)} copy(f32[1024,768]{0,1:T(8,128)} %fusion.17) | data formatting | bytes 6291456
  (448 shorter events, 209.4 us)
Async XLA Ops:
  65.9 26.5 %collective-permute-start.2 = (f32[1024,768]{0,1:T(8,128)}, f32[1024,768]{0,1:T(8,128)S(1)}, u32[]{:S(2)}, u32[]{:S(2)}) collective-permute-start(f32[1024,768]{0,1:T(8,128)} %copy.55), channel_id=1, source_target_pairs={{0,1},{1,0},{2,3},{3,2},{4,5},{5,4},{6,7},{7,6},{8,9},{9,8},{10,11... | collective-permute-start | bytes 9437192 | tf_op jit(solution)/shard_map/ppermute | solution.py:64
  71.0 23.3 %collective-permute-start.1 = (f32[1024,768]{0,1:T(8,128)S(1)}, f32[1024,768]{0,1:T(8,128)S(1)}, u32[]{:S(2)}, u32[]{:S(2)}) collective-permute-start(f32[1024,768]{0,1:T(8,128)S(1)} %fusion.71), channel_id=1, source_target_pairs={{0,1},{1,0},{2,3},{3,2},{4,5},{5,4},{6,7},{7,6},{8,9},{9,8},{10,11... | collective-permute-start | bytes 9437192 | tf_op jit(solution)/shard_map/ppermute | solution.py:64
  80.9 21.5 %collective-permute-start.45 = (f32[2,2,2,48,512]{4,3,1,0,2:T(8,128)}, f32[2,2,2,48,512]{4,3,1,0,2:T(8,128)}, u32[]{:S(2)}, u32[]{:S(2)}) collective-permute-start(f32[2,2,2,48,512]{4,3,1,0,2:T(8,128)} %bitcast.272), channel_id=1, source_target_pairs={{0,2},{2,0},{4,6},{6,4},{8,10},{10,8},{12,14},{14,12},{16,18},{18,... | collective-permute-start | bytes 2359304 | tf_op jit(solution)/shard_map/ppermute | solution.py:64
  85.1 23.9 %collective-permute-start.49 = (f32[2,2,2,48,512]{4,3,1,0,2:T(8,128)}, f32[2,2,2,48,512]{4,3,1,0,2:T(8,128)}, u32[]{:S(2)}, u32[]{:S(2)}) collective-permute-start(f32[2,2,2,48,512]{4,3,1,0,2:T(8,128)} %bitcast.271), channel_id=1, source_target_pairs={{0,4},{2,6},{4,0},{6,2},{8,12},{10,14},{12,8},{14,10},{16,20},{18,... | collective-permute-start | bytes 2359304 | tf_op jit(solution)/shard_map/ppermute | solution.py:64
  88.8 25.5 %collective-permute-start.53 = (f32[2,2,2,48,512]{4,3,1,0,2:T(8,128)}, f32[2,2,2,48,512]{4,3,1,0,2:T(8,128)}, u32[]{:S(2)}, u32[]{:S(2)}) collective-permute-start(f32[2,2,2,48,512]{4,3,1,0,2:T(8,128)} %bitcast.270), channel_id=1, source_target_pairs={{0,8},{2,10},{4,12},{6,14},{8,0},{10,2},{12,4},{14,6},{16,24},{18,... | collective-permute-start | bytes 2359304 | tf_op jit(solution)/shard_map/ppermute | solution.py:64
  92.4 32.2 %collective-permute-start.33 = (f32[2,2,2,48,512]{4,3,1,0,2:T(8,128)}, f32[2,2,2,48,512]{4,3,1,0,2:T(8,128)}, u32[]{:S(2)}, u32[]{:S(2)}) collective-permute-start(f32[2,2,2,48,512]{4,3,1,0,2:T(8,128)} %bitcast.275), channel_id=1, source_target_pairs={{0,2},{2,0},{4,6},{6,4},{8,10},{10,8},{12,14},{14,12},{16,18},{18,... | collective-permute-start | bytes 2359304 | tf_op jit(solution)/shard_map/ppermute | solution.py:64
  94.3 51.7 %collective-permute-start.37 = (f32[2,2,2,48,512]{4,3,1,0,2:T(8,128)}, f32[2,2,2,48,512]{4,3,1,0,2:T(8,128)}, u32[]{:S(2)}, u32[]{:S(2)}) collective-permute-start(f32[2,2,2,48,512]{4,3,1,0,2:T(8,128)} %bitcast.274), channel_id=1, source_target_pairs={{0,4},{2,6},{4,0},{6,2},{8,12},{10,14},{12,8},{14,10},{16,20},{18,... | collective-permute-start | bytes 2359304 | tf_op jit(solution)/shard_map/ppermute | solution.py:64
  102.4 51.5 %collective-permute-start.41 = (f32[2,2,2,48,512]{4,3,1,0,2:T(8,128)S(1)}, f32[2,2,2,48,512]{4,3,1,0,2:T(8,128)S(1)}, u32[]{:S(2)}, u32[]{:S(2)}) collective-permute-start(f32[2,2,2,48,512]{4,3,1,0,2:T(8,128)S(1)} %bitcast.300), channel_id=1, source_target_pairs={{0,8},{2,10},{4,12},{6,14},{8,0},{10,2},{12,4},{14,6},{16,24},{18,... | collective-permute-start | bytes 2359304 | tf_op jit(solution)/shard_map/ppermute | solution.py:64
  109.0 117.1 %collective-permute-start.46 = (f32[2,2,48,512]{3,2,1,0:T(8,128)}, f32[2,2,48,512]{3,2,1,0:T(8,128)}, u32[]{:S(2)}, u32[]{:S(2)}) collective-permute-start(f32[2,2,48,512]{3,2,1,0:T(8,128)} %dynamic-slice_bitcast_fusion.2), channel_id=1, source_target_pairs={{0,4},{2,6},{4,0},{6,2},{8,12},{10,14},{12,8},{14,10},{16,20},{18,... | collective-permute-start | bytes 1179656 | tf_op jit(solution)/shard_map/ppermute | solution.py:64
  114.3 114.0 %collective-permute-start.50 = (f32[2,2,48,512]{3,2,1,0:T(8,128)}, f32[2,2,48,512]{3,2,1,0:T(8,128)}, u32[]{:S(2)}, u32[]{:S(2)}) collective-permute-start(f32[2,2,48,512]{3,2,1,0:T(8,128)} %dynamic-slice_bitcast_fusion.1), channel_id=1, source_target_pairs={{0,2},{2,0},{4,6},{6,4},{8,10},{10,8},{12,14},{14,12},{16,18},{18,... | collective-permute-start | bytes 1179656 | tf_op jit(solution)/shard_map/ppermute | solution.py:64
  124.6 105.8 %collective-permute-start.54 = (f32[2,2,48,512]{3,2,1,0:T(8,128)}, f32[2,2,48,512]{3,2,1,0:T(8,128)}, u32[]{:S(2)}, u32[]{:S(2)}) collective-permute-start(f32[2,2,48,512]{3,2,1,0:T(8,128)} %dynamic-slice_bitcast_fusion), channel_id=1, source_target_pairs={{0,2},{2,0},{4,6},{6,4},{8,10},{10,8},{12,14},{14,12},{16,18},{18,... | collective-permute-start | bytes 1179656 | tf_op jit(solution)/shard_map/ppermute | solution.py:64
  146.0 85.8 %collective-permute-start.34 = (f32[2,2,48,512]{3,2,1,0:T(8,128)}, f32[2,2,48,512]{3,2,1,0:T(8,128)}, u32[]{:S(2)}, u32[]{:S(2)}) collective-permute-start(f32[2,2,48,512]{3,2,1,0:T(8,128)} %dynamic-slice_bitcast_fusion.5), channel_id=1, source_target_pairs={{0,4},{2,6},{4,0},{6,2},{8,12},{10,14},{12,8},{14,10},{16,20},{18,... | collective-permute-start | bytes 1179656 | tf_op jit(solution)/shard_map/ppermute | solution.py:64
  158.2 13.9 %collective-permute-start.17 = (f32[2,2,2,48,128]{4,3,1,0,2:T(8,128)}, f32[2,2,2,48,128]{4,3,1,0,2:T(8,128)}, u32[]{:S(2)}, u32[]{:S(2)}) collective-permute-start(f32[2,2,2,48,128]{4,3,1,0,2:T(8,128)} %bitcast.281), channel_id=1, source_target_pairs={{0,2},{2,0},{4,6},{6,4},{8,10},{10,8},{12,14},{14,12},{16,18},{18,... | collective-permute-start | bytes 589832 | tf_op jit(solution)/shard_map/ppermute | solution.py:64
  228.4 25.7 %collective-permute-start.29 = (f32[2,2,2,48,384]{4,3,1,0,2:T(8,128)S(1)}, f32[2,2,2,48,384]{4,3,1,0,2:T(8,128)S(1)}, u32[]{:S(2)}, u32[]{:S(2)}) collective-permute-start(f32[2,2,2,48,384]{4,3,1,0,2:T(8,128)S(1)} %bitcast.301), channel_id=1, source_target_pairs={{0,2},{2,0},{4,6},{6,4},{8,10},{10,8},{12,14},{14,12},{16,18},{18,... | collective-permute-start | bytes 1769480 | tf_op jit(solution)/shard_map/ppermute | solution.py:64
  230.3 24.4 %collective-permute-start.13 = (f32[2,2,2,48,384]{4,3,1,0,2:T(8,128)S(1)}, f32[2,2,2,48,384]{4,3,1,0,2:T(8,128)S(1)}, u32[]{:S(2)}, u32[]{:S(2)}) collective-permute-start(f32[2,2,2,48,384]{4,3,1,0,2:T(8,128)S(1)} %bitcast.303), channel_id=1, source_target_pairs={{0,8},{2,10},{4,12},{6,14},{8,0},{10,2},{12,4},{14,6},{16,24},{18,... | collective-permute-start | bytes 1769480 | tf_op jit(solution)/shard_map/ppermute | solution.py:64
  248.1 46.4 %collective-permute-start.3 = (f32[1024,768]{0,1:T(8,128)S(1)}, f32[1024,768]{0,1:T(8,128)S(1)}, u32[]{:S(2)}, u32[]{:S(2)}) collective-permute-start(f32[1024,768]{0,1:T(8,128)S(1)} %add_add_fusion), channel_id=1, source_target_pairs={{0,1},{1,0},{2,3},{3,2},{4,5},{5,4},{6,7},{7,6},{8,9},{9,8},{10,11... | collective-permute-start | bytes 9437192 | tf_op jit(solution)/shard_map/ppermute | solution.py:64
  250.2 13.6 %collective-permute-start.9 = (f32[2,2,2,48,384]{4,3,1,0,2:T(8,128)S(1)}, f32[2,2,2,48,384]{4,3,1,0,2:T(8,128)S(1)}, u32[]{:S(2)}, u32[]{:S(2)}) collective-permute-start(f32[2,2,2,48,384]{4,3,1,0,2:T(8,128)S(1)} %bitcast.302), channel_id=1, source_target_pairs={{0,4},{2,6},{4,0},{6,2},{8,12},{10,14},{12,8},{14,10},{16,20},{18,... | collective-permute-start | bytes 1769480 | tf_op jit(solution)/shard_map/ppermute | solution.py:64
  251.5 15.1 %collective-permute-start.48 = (f32[48,512]{1,0:T(8,128)S(1)}, f32[48,512]{1,0:T(8,128)S(1)}, u32[]{:S(2)}, u32[]{:S(2)}) collective-permute-start(f32[48,512]{1,0:T(8,128)S(1)} %dynamic-slice_bitcast_fusion.20), channel_id=1, source_target_pairs={{0,16},{2,18},{4,20},{6,22},{8,24},{10,26},{12,28},{14,30},{16,0},... | collective-permute-start | bytes 294920 | tf_op jit(solution)/shard_map/ppermute | solution.py:64
  254.1 12.9 %collective-permute-start.52 = (f32[48,512]{1,0:T(8,128)S(1)}, f32[48,512]{1,0:T(8,128)S(1)}, u32[]{:S(2)}, u32[]{:S(2)}) collective-permute-start(f32[48,512]{1,0:T(8,128)S(1)} %dynamic-slice_bitcast_fusion.19), channel_id=1, source_target_pairs={{0,16},{2,18},{4,20},{6,22},{8,24},{10,26},{12,28},{14,30},{16,0},... | collective-permute-start | bytes 294920 | tf_op jit(solution)/shard_map/ppermute | solution.py:64
  254.7 14.9 %collective-permute-start.56 = (f32[48,512]{1,0:T(8,128)S(1)}, f32[48,512]{1,0:T(8,128)S(1)}, u32[]{:S(2)}, u32[]{:S(2)}) collective-permute-start(f32[48,512]{1,0:T(8,128)S(1)} %dynamic-slice_bitcast_fusion.18), channel_id=1, source_target_pairs={{0,16},{2,18},{4,20},{6,22},{8,24},{10,26},{12,28},{14,30},{16,0},... | collective-permute-start | bytes 294920 | tf_op jit(solution)/shard_map/ppermute | solution.py:64
  263.8 11.9 %collective-permute-start.36 = (f32[48,512]{1,0:T(8,128)S(1)}, f32[48,512]{1,0:T(8,128)S(1)}, u32[]{:S(2)}, u32[]{:S(2)}) collective-permute-start(f32[48,512]{1,0:T(8,128)S(1)} %dynamic-slice_bitcast_fusion.23), channel_id=1, source_target_pairs={{0,16},{2,18},{4,20},{6,22},{8,24},{10,26},{12,28},{14,30},{16,0},... | collective-permute-start | bytes 294920 | tf_op jit(solution)/shard_map/ppermute | solution.py:64
  267.0 11.6 %collective-permute-start.44 = (f32[48,512]{1,0:T(8,128)S(1)}, f32[48,512]{1,0:T(8,128)S(1)}, u32[]{:S(2)}, u32[]{:S(2)}) collective-permute-start(f32[48,512]{1,0:T(8,128)S(1)} %dynamic-slice_bitcast_fusion.21), channel_id=1, source_target_pairs={{0,16},{2,18},{4,20},{6,22},{8,24},{10,26},{12,28},{14,30},{16,0},... | collective-permute-start | bytes 294920 | tf_op jit(solution)/shard_map/ppermute | solution.py:64
  294.4 13.4 %collective-permute-start.12 = (f32[48,384]{1,0:T(8,128)S(1)}, f32[48,384]{1,0:T(8,128)S(1)}, u32[]{:S(2)}, u32[]{:S(2)}) collective-permute-start(f32[48,384]{1,0:T(8,128)S(1)} %dynamic-slice_bitcast_fusion.29), channel_id=1, source_target_pairs={{0,16},{2,18},{4,20},{6,22},{8,24},{10,26},{12,28},{14,30},{16,0},... | collective-permute-start | bytes 221192 | tf_op jit(solution)/shard_map/ppermute | solution.py:64
  320.1 12.1 %collective-permute-start.8 = (f32[441,128]{1,0:T(8,128)S(1)}, f32[441,128]{1,0:T(8,128)S(1)}, u32[]{:S(2)}, u32[]{:S(2)}) collective-permute-start(f32[441,128]{1,0:T(8,128)S(1)} %add.466), channel_id=1, source_target_pairs={{0,16},{2,18},{4,20},{6,22},{8,24},{10,26},{12,28},{14,30},{16,0},... | collective-permute-start | bytes 677384 | tf_op jit(solution)/shard_map/ppermute | solution.py:64
  (114 other events, 1011.5 us)
